TPU v7x, 32 devices: a whole 2x2x4 slice. The times are simulated.
32 devices in a mesh: dp: 8 (over z, x), expert: 4 (over y, core).
Axes of the slice: x: 2, y: 2, z: 4, core: 2. Of those that a mesh axis runs over, the one named last changes fastest.
Arguments:
- layer_in: bfloat16 [8192, 1024], P(('dp', 'expert')), may hold values from -6 to 6
- body_of: int32 [8192], P(('dp', 'expert')), may hold values from 0 to 5, as said below
- expert_of: int32 [8192, 1], P(('dp', 'expert')), may hold values from 0 to 7; in each aligned block of 256 rows (0 to 255, 256 to 511, ...) at most 48 rows name the same one
- w_qkv: bfloat16 [1024, 1536], replicated, may hold values from -0.1875 to 0.1875
- w_o: bfloat16 [1024, 512], replicated, may hold values from -0.25 to 0.25
- w_up: bfloat16 [8, 1024, 1024], P('expert', None, 'dp'), may hold values from -0.1875 to 0.1875
- w_down: bfloat16 [8, 1024, 1024], P('expert', 'dp'), may hold values from -0.1875 to 0.1875
- d_out: bfloat16 [8192, 1024], P(('dp', 'expert')), may hold values from -6 to 6
Outputs:
- out: bfloat16 [8192, 1024], P(('dp', 'expert'))
- grad_input: bfloat16 [8192, 1024], P(('dp', 'expert'))
- grad_qkv: float32 [1024, 1536], P(('dp', 'expert'))
- grad_o: float32 [1024, 512], P(('dp', 'expert'))
- grad_up: float32 [8, 1024, 1024], P('expert', None, 'dp')
- grad_down: float32 [8, 1024, 1024], P('expert', 'dp')
Inputs may be any that keep to these rules, and one draw needn't show every extreme that they name: `body_of`: within each device's 256 rows the ids start at 0 and rise by one at each new body; every body has 16 to 128 tokens, no body crosses a multiple of 128 rows of its device, no block of 128 rows holds more than 3 bodies, and some device holds 3 bodies in each of its blocks. `expert_of`: in the 256 rows of one device no expert is named more than 48 times, a bound that some block reaches.
All inputs are finite; a program needn't handle non-finite values.
Results may differ from a plain program's by a relative error of at most 0.014.
Values may be sent and summed in bfloat16 or wider, within the bound.
A program may use at most 128 MiB of HBM per device.

v0:
```python
import jax
import jax.numpy as jnp
from jax import lax
from jax.sharding import PartitionSpec as P

HD = 64
EPSILON = 1e-06


def rms_norm(values):
    scale = lax.rsqrt(jnp.mean(values * values, axis=-1, keepdims=True) + EPSILON)
    return (values * scale).astype(jnp.bfloat16)


def gelu_tanh(values):
    return jax.nn.gelu(values, approximate=True)


def gelu_back(pre_act, cotangent):
    return jax.vjp(gelu_tanh, pre_act)[1](cotangent)[0]


def row_contract(left, right):
    return lax.dot_general(
        left, right, (((0,), (0,)), ((), ())), preferred_element_type=jnp.float32
    )


def col_contract(left, right):
    return lax.dot_general(
        left, right, (((1,), (1,)), ((), ())), preferred_element_type=jnp.float32
    )


def attention_core(packed, labels_row):
    rows = packed.shape[0]
    blocks = rows // 128
    width = packed.shape[1] // 3
    heads = width // HD
    parts = packed.reshape(blocks, 128, 3, heads, HD)
    query = parts[:, :, 0]
    keys = parts[:, :, 1]
    values = parts[:, :, 2]
    scores = jnp.einsum(
        "bqhc,bkhc->bhqk", query, keys, preferred_element_type=jnp.float32
    ) * HD ** (-0.5)
    labels = labels_row.reshape(blocks, 128)
    same = (labels[:, :, None] == labels[:, None, :])[:, None]
    weights = jnp.where(same, jnp.exp(scores), 0.0)
    probs = (weights / jnp.sum(weights, axis=-1, keepdims=True)).astype(jnp.bfloat16)
    mixed = jnp.einsum("bhqk,bkhc->bqhc", probs, values, preferred_element_type=jnp.float32)
    return mixed.astype(jnp.bfloat16).reshape(rows, width)


def on_device(layer_in, body_of, expert_of, w_qkv, w_o, w_up, w_down, d_out):
    tok_rows = layer_in.shape[0]
    width = layer_in.shape[1]
    shards = lax.axis_size("expert")
    local_experts = w_up.shape[0]
    all_experts = local_experts * shards
    capacity = 3 * tok_rows // (2 * all_experts)
    received = shards * capacity
    layer_f = layer_in.astype(jnp.float32)
    normed, norm_x_back = jax.vjp(rms_norm, layer_f)
    packed = jnp.dot(normed, w_qkv, preferred_element_type=jnp.float32).astype(jnp.bfloat16)
    mixed, core_back = jax.vjp(lambda value: attention_core(value, body_of), packed)
    resid = (layer_f + col_contract(mixed, w_o)).astype(jnp.bfloat16)
    inner, norm_h_back = jax.vjp(rms_norm, resid.astype(jnp.float32))
    expert_ids = expert_of[:, 0]
    onehot = (expert_ids[:, None] == jnp.arange(all_experts, dtype=jnp.int32)[None, :]).astype(
        jnp.int32
    )
    ranks = jnp.sum(jnp.cumsum(onehot, axis=0) * onehot, axis=-1) - 1
    slots = expert_ids * capacity + ranks

    def to_slots(values):
        store = jnp.zeros((all_experts * capacity, width), values.dtype).at[slots].set(values)
        return store.reshape(shards, local_experts, capacity, width)

    sent_inner = lax.all_to_all(to_slots(inner), "expert", split_axis=0, concat_axis=2, tiled=True)
    inputs = sent_inner.reshape(local_experts, received, width)
    full_up, full_down = (
        lax.all_gather(w_up, "dp", axis=2, tiled=True),
        lax.all_gather(w_down, "dp", axis=1, tiled=True),
    )
    pre_act = jnp.einsum("esd,edf->esf", inputs, full_up, preferred_element_type=jnp.float32)
    hidden = gelu_tanh(pre_act).astype(jnp.bfloat16)
    result = jnp.einsum("esf,efd->esd", hidden, full_down, preferred_element_type=jnp.float32)
    outgoing = result.astype(jnp.bfloat16).reshape(1, local_experts, received, width)
    returned = lax.all_to_all(outgoing, "expert", split_axis=2, concat_axis=0, tiled=True)
    expert_out = returned.reshape(all_experts * capacity, width)[slots]
    out = (resid.astype(jnp.float32) + expert_out.astype(jnp.float32)).astype(jnp.bfloat16)
    sent_grads = lax.all_to_all(to_slots(d_out), "expert", split_axis=0, concat_axis=2, tiled=True)
    grads_in = sent_grads.reshape(local_experts, received, width)
    d_hidden = jnp.einsum("esd,efd->esf", grads_in, full_down, preferred_element_type=jnp.float32)
    d_pre = gelu_back(pre_act, d_hidden).astype(jnp.bfloat16)
    part_up = jnp.einsum("esd,esf->edf", inputs, d_pre, preferred_element_type=jnp.float32)
    part_down = jnp.einsum("esf,esd->efd", hidden, grads_in, preferred_element_type=jnp.float32)
    d_inputs = jnp.einsum("esf,edf->esd", d_pre, full_up, preferred_element_type=jnp.float32)
    going_back = d_inputs.astype(jnp.bfloat16).reshape(1, local_experts, received, width)
    came_back = lax.all_to_all(going_back, "expert", split_axis=2, concat_axis=0, tiled=True)
    d_inner = came_back.reshape(all_experts * capacity, width)[slots]
    grad_up, grad_down = (
        lax.psum_scatter(
            part_up.astype(jnp.bfloat16), "dp", scatter_dimension=2, tiled=True
        ).astype(jnp.float32),
        lax.psum_scatter(
            part_down.astype(jnp.bfloat16), "dp", scatter_dimension=1, tiled=True
        ).astype(jnp.float32),
    )
    d_resid = (d_out.astype(jnp.float32) + norm_h_back(d_inner)[0]).astype(jnp.bfloat16)
    term_o = row_contract(d_resid, mixed)
    d_mixed = jnp.dot(d_resid, w_o, preferred_element_type=jnp.float32).astype(jnp.bfloat16)
    d_packed = core_back(d_mixed)[0]
    term_qkv = row_contract(normed, d_packed)
    grad_qkv, grad_o = (
        lax.psum_scatter(term_qkv, ("dp", "expert"), scatter_dimension=0, tiled=True),
        lax.psum_scatter(term_o, ("dp", "expert"), scatter_dimension=0, tiled=True),
    )
    d_normed = col_contract(d_packed, w_qkv).astype(jnp.bfloat16)
    grad_input = (d_resid.astype(jnp.float32) + norm_x_back(d_normed)[0]).astype(jnp.bfloat16)
    return (out, grad_input, grad_qkv, grad_o, grad_up, grad_down)


def solution(mesh):
    in_specs = (
        P(("dp", "expert"), None),
        P(("dp", "expert")),
        P(("dp", "expert"), None),
        P(),
        P(),
        P("expert", None, "dp"),
        P("expert", "dp", None),
        P(("dp", "expert"), None),
    )
    out_specs = (
        P(("dp", "expert"), None),
        P(("dp", "expert"), None),
        P(("dp", "expert"), None),
        P(("dp", "expert"), None),
        P("expert", None, "dp"),
        P("expert", "dp", None),
    )
    return jax.shard_map(
        on_device, mesh=mesh, in_specs=in_specs, out_specs=out_specs, check_vma=False
    )
```

profile of v0, /device:TPU:0, one launch (start us, length us, event | category | flops | bytes accessed | tf_op | source)
XLA Modules:
  0.0 630.3 jit_solution(3287069089571837965)
XLA Ops:
  14.7 4.2 all-to-all-start.2
  42.3 4.2 all-to-all-start
  48.9 9.9 %all-to-all-done = bf16[4,2,48,1024]{3,2,1,0:T(8,128)(2,1)} async-done(((bf16[4,2,48,1024]{3,2,1,0:T(8,128)(2,1)}), bf16[4,2,48,1024]{3,2,1,0:T(8,128)(2,1)}, u32[]{:S(2)}, u32[]{:S(2)}) %all-to-all-start) | async-done | bytes 786464 | tf_op jit(solution)/shard_map/all_to_all | solution.py:80
  60.9 25.4 %all-gather.5.cloned.1.call-done = bf16[2,1024,1024]{2,1,0:T(8,128)(2,1)} async-done(((bf16[2,128,1024]{2,1,0:T(8,128)(2,1)}), bf16[2,1024,1024]{2,1,0:T(8,128)(2,1)}) %all-gather.5.cloned.1.call-update) | async-done | bytes 4194320 | tf_op jit(solution)/shard_map/all_gather | solution.py:84
  86.3 5.1 fusion.65
  91.4 70.3 %all-gather.3.cloned.1.call-done = bf16[2,1024,1024]{2,1,0:T(8,128)(2,1)} async-done(((bf16[2,1024,128]{2,1,0:T(8,128)(2,1)}), bf16[2,1024,1024]{2,1,0:T(8,128)(2,1)}) %all-gather.3.cloned.1.call-update) | async-done | bytes 4194320 | tf_op jit(solution)/shard_map/all_gather | solution.py:83
  161.7 6.0 fusion.6
  168.5 3.2 convolution_convert_fusion.1
  171.7 11.3 %copy.64 = bf16[2,1024,1024]{1,0,2:T(2,128)(2,1)} copy(bf16[2,1024,1024]{2,1,0:T(8,128)(2,1)} %convolution_convert_fusion.1) | data formatting | bytes 8388608
  183.1 5.6 copy.73
  188.7 4.9 convolution_convert_fusion
  193.6 4.1 fusion.9
  199.4 4.2 all-to-all-start.3
  203.6 3.9 fusion.8
  209.2 6.1 all-to-all-done.3
  215.3 4.2 all-to-all-start.1
  222.0 9.2 %all-to-all-done.1 = bf16[1,2,192,1024]{3,1,0,2:T(2,128)(2,1)} async-done(((bf16[1,2,192,1024]{3,1,0,2:T(2,128)(2,1)}), bf16[1,2,192,1024]{3,1,0,2:T(2,128)(2,1)}, u32[]{:S(2)}, u32[]{:S(2)}) %all-to-all-start.1) | async-done | bytes 786464 | tf_op jit(solution)/shard_map/all_to_all | solution.py:90
  233.5 3.6 gather_fusion.1
  237.1 3.6 gather_fusion
  259.6 3.8 fusion.32
  267.1 7.8 %reduce-scatter.13.cloned.1.call-done = bf16[128,2048]{1,0:T(8,128)(2,1)} async-done(((bf16[1024,2048]{1,0:T(8,128)(2,1)}), bf16[128,2048]{1,0:T(8,128)(2,1)}) %reduce-scatter.13.cloned.1.call-update) | async-done | bytes 524304
  281.2 85.5 %reduce-scatter.11.cloned.1.call-done = bf16[2,128,1024]{2,1,0:T(8,128)(2,1)} async-done(((bf16[2,1024,1024]{2,1,0:T(8,128)(2,1)}), bf16[2,128,1024]{2,1,0:T(8,128)(2,1)}) %reduce-scatter.11.cloned.1.call-update) | async-done | bytes 524304 | tf_op jit(solution)/shard_map/reduce_scatter | solution.py:107
  368.8 137.2 %reduce-scatter.9.cloned.1.call-done = f32[32,512]{1,0:T(8,128)} async-done(((f32[1024,512]{1,0:T(8,128)}), f32[32,512]{1,0:T(8,128)}) %reduce-scatter.9.cloned.1.call-update) | async-done | bytes 65552 | tf_op jit(solution)/shard_map/reduce_scatter | solution.py:118
  506.0 117.4 %reduce-scatter.7.cloned.1.call-done = f32[32,1536]{1,0:T(8,128)} async-done(((f32[1024,1536]{1,0:T(8,128)}), f32[32,1536]{1,0:T(8,128)}) %reduce-scatter.7.cloned.1.call-update) | async-done | bytes 196624 | tf_op jit(solution)/shard_map/reduce_scatter | solution.py:117
  (107 shorter events, 75.2 us)
Async XLA Ops:
  7.2 13.1 %copy-start = (bf16[1024,1536]{1,0:T(8,128)(2,1)S(1)}, bf16[1024,1536]{1,0:T(8,128)(2,1)}, u32[]{:S(2)}) copy-start(bf16[1024,1536]{1,0:T(8,128)(2,1)} %param.11) | copy-start | bytes 9437188
  7.2 79.1 %all-gather.5.cloned.1.call-start = ((), (), s32[]{:S(2)}) async-start(), calls=%async_computation.9 | async-start | bytes 4718592 | tf_op jit(solution)/shard_map/all_gather | solution.py:84
  7.9 153.8 %all-gather.3.cloned.1.call-start = ((), (), s32[]{:S(2)}) async-start(), calls=%async_computation.8 | async-start | bytes 4718592 | tf_op jit(solution)/shard_map/all_gather | solution.py:83
  14.7 27.6 %all-to-all-start.2 = ((bf16[4,2,48,1024]{3,2,1,0:T(8,128)(2,1)}), bf16[4,2,48,1024]{3,2,1,0:T(8,128)(2,1)}, u32[]{:S(2)}, u32[]{:S(2)}) async-start(bf16[4,2,48,1024]{3,2,1,0:T(8,128)(2,1)} %bitcast.121), calls=%async_computation.2 | async-start | bytes 1572864 | tf_op jit(solution)/shard_map/all_to_all | solution.py:93
  28.9 5.4 copy-start.19
  35.8 1.5 copy-start.3
  35.9 1.9 copy-start.14
  37.4 1.7 copy-start.15
  42.3 16.5 %all-to-all-start = ((bf16[4,2,48,1024]{3,2,1,0:T(8,128)(2,1)}), bf16[4,2,48,1024]{3,2,1,0:T(8,128)(2,1)}, u32[]{:S(2)}, u32[]{:S(2)}) async-start(bf16[4,2,48,1024]{3,2,1,0:T(8,128)(2,1)} %bitcast.122), calls=%async_computation | async-start | bytes 1572864 | tf_op jit(solution)/shard_map/all_to_all | solution.py:80
  46.5 228.4 %reduce-scatter.13.cloned.1.call-start = ((), (), s32[]{:S(2)}) async-start(), calls=%async_computation.13 | async-start | bytes 4718592
  161.7 6.8 %copy-start.10 = (bf16[1,2,4,48,1024]{4,3,2,1,0:T(8,128)(2,1)S(1)}, bf16[1,2,4,48,1024]{4,3,2,1,0:T(8,128)(2,1)}, u32[]{:S(2)}) copy-start(bf16[1,2,4,48,1024]{4,3,2,1,0:T(8,128)(2,1)} %copy.47) | copy-start | bytes 2359300
  188.6 178.1 %reduce-scatter.11.cloned.1.call-start = ((), (), s32[]{:S(2)}) async-start(), calls=%async_computation.12 | async-start | bytes 4718592 | tf_op jit(solution)/shard_map/reduce_scatter | solution.py:107
  199.4 15.9 %all-to-all-start.3 = ((bf16[1,2,192,1024]{3,1,0,2:T(2,128)(2,1)}), bf16[1,2,192,1024]{3,1,0,2:T(2,128)(2,1)}, u32[]{:S(2)}, u32[]{:S(2)}) async-start(bf16[1,2,192,1024]{3,1,0,2:T(2,128)(2,1)} %copy.51), calls=%async_computation.3 | async-start | bytes 1572864 | tf_op jit(solution)/shard_map/all_to_all | solution.py:101
  215.3 15.9 %all-to-all-start.1 = ((bf16[1,2,192,1024]{3,1,0,2:T(2,128)(2,1)}), bf16[1,2,192,1024]{3,1,0,2:T(2,128)(2,1)}, u32[]{:S(2)}, u32[]{:S(2)}) async-start(bf16[1,2,192,1024]{3,1,0,2:T(2,128)(2,1)} %copy.48), calls=%async_computation.1 | async-start | bytes 1572864 | tf_op jit(solution)/shard_map/all_to_all | solution.py:90
  219.5 286.5 %reduce-scatter.9.cloned.1.call-start = ((), (), s32[]{:S(2)}) async-start(), calls=%async_computation.11 | async-start | bytes 2162688 | tf_op jit(solution)/shard_map/reduce_scatter | solution.py:118
  242.1 3.6 copy-start.16
  247.6 375.9 %reduce-scatter.7.cloned.1.call-start = ((), (), s32[]{:S(2)}) async-start(), calls=%async_computation.10 | async-start | bytes 6488064 | tf_op jit(solution)/shard_map/reduce_scatter | solution.py:117
  253.7 2.2 copy-start.7
  253.7 2.2 copy-start.13
  253.7 2.7 copy-start.9
  253.7 2.7 copy-start.17
  257.8 1.8 copy-start.4
  263.4 2.5 copy-start.2
  263.4 2.5 copy-start.5
  (6 other events, 5.8 us)
Sparse Core Ops, SparseCore 0:
  10.2 76.0 all-gather.4
  88.3 73.2 all-gather.2
  188.8 86.0 reduce-scatter.12
  278.8 87.8 reduce-scatter.10
  369.4 136.5 reduce-scatter.8
  513.0 110.3 reduce-scatter.6
where the time goes:
time: 632 us; the launch traced here: 630 us
  waiting for transfers between devices  470 us (74%)
  local copies, waits for them, and re-layouts  63.7 us (10%)
  matrix products  47.3 us (7%)
  starting transfers between devices  17.5 us (3%)
  other arithmetic  17.1 us (3%)
  between operations  14.5 us (2%)
    reduce_scatter x1, waiting for transfers between devices, on_device(): lax.psum_scatter(term_o, ('dp', 'expert'), scatter_dimension=0, tiled=True)  137 us
    reduce_scatter x1, waiting for transfers between devices, on_device(): lax.psum_scatter(term_qkv, ('dp', 'expert'), scatter_dimension=0, tiled=T...  117 us
    reduce_scatter x1, waiting for transfers between devices, on_device(): lax.psum_scatter(part_down.astype(jnp.bfloat16), 'dp', scatter_dimension=...  85.5 us
    all_gather x1, waiting for transfers between devices, on_device(): lax.all_gather(w_up, 'dp', axis=2, tiled=True)  70.3 us
    unnamed x47, local copies, waits for them, and re-layouts  30.8 us
    all_gather x1, waiting for transfers between devices, on_device(): lax.all_gather(w_down, 'dp', axis=1, tiled=True)  25.4 us
  transfers between devices with their start and end apart: 10, of which 9 were waited for; matrix products, arithmetic and copies ran while one was open for 16% of the time, Pallas kernels for 0%

commit v1 on v0

--- a/solution.py
+++ b/solution.py
@@ -5,6 +5,18 @@
 
 HD = 64
 EPSILON = 1e-06
+
+
+def doubled_up(x, axis, dim):
+    ways, here = (lax.axis_size(axis), lax.axis_index(axis))
+    grown, reach = (x, 1)
+    while reach < ways:
+        theirs = lax.ppermute(grown, axis, [(d, d ^ reach) for d in range(ways)])
+        mine_first = jnp.concatenate([grown, theirs], axis=dim)
+        theirs_first = jnp.concatenate([theirs, grown], axis=dim)
+        grown = jnp.where(here & reach == 0, mine_first, theirs_first)
+        reach = 2 * reach
+    return grown
 
 
 def rms_norm(values):
@@ -80,7 +92,7 @@
     sent_inner = lax.all_to_all(to_slots(inner), "expert", split_axis=0, concat_axis=2, tiled=True)
     inputs = sent_inner.reshape(local_experts, received, width)
     full_up, full_down = (
-        lax.all_gather(w_up, "dp", axis=2, tiled=True),
+        doubled_up(w_up, "dp", 2),
         lax.all_gather(w_down, "dp", axis=1, tiled=True),
     )
     pre_act = jnp.einsum("esd,edf->esf", inputs, full_up, preferred_element_type=jnp.float32)

time: 632 us -> 657 us (1.040)
  waiting for transfers between devices: 470 us -> 484 us
  other arithmetic: 17.1 us -> 25.6 us
    ppermute x0 -> x3, waiting for transfers between devices: none -> 70.5 us  [doubled_up(): theirs = lax.ppermute(grown, axis, [(d, d ^ reach) for d in range(ways)])]
    all_gather x1 -> x0, waiting for transfers between devices: 70.3 us -> none  [on_device(): lax.all_gather(w_up, 'dp', axis=2, tiled=True)]
    all_gather x1, waiting for transfers between devices: 25.4 us -> 41.5 us  [on_device(): lax.all_gather(w_down, 'dp', axis=1, tiled=True)]
    select_n x0 -> x2, other arithmetic: none -> 7.12 us  [doubled_up(): grown = jnp.where(here & reach == 0, mine_first, theirs_first)]
    unnamed x47 -> x51, local copies, waits for them, and re-layouts: 30.8 us -> 30 us
  transfers between devices with their start and end apart: 10 -> 12, of which waited for: 9 -> 11; matrix products, arithmetic and copies ran while one was open for 16% -> 16% of each run, Pallas kernels for 0% -> 0%
where the time goes in v1:
time: 657 us; the launch traced here: 655 us
  waiting for transfers between devices  484 us (74%)
  local copies, waits for them, and re-layouts  62.7 us (10%)
  matrix products  46.7 us (7%)
  other arithmetic  25.6 us (4%)
  starting transfers between devices  21.6 us (3%)
  between operations  14.1 us (2%)
    reduce_scatter x1, waiting for transfers between devices, on_device(): lax.psum_scatter(term_o, ('dp', 'expert'), scatter_dimension=0, tiled=True)  137 us
    reduce_scatter x1, waiting for transfers between devices, on_device(): lax.psum_scatter(term_qkv, ('dp', 'expert'), scatter_dimension=0, tiled=T...  117 us
    reduce_scatter x1, waiting for transfers between devices, on_device(): lax.psum_scatter(part_down.astype(jnp.bfloat16), 'dp', scatter_dimension=...  85.4 us
    ppermute x3, waiting for transfers between devices, doubled_up(): theirs = lax.ppermute(grown, axis, [(d, d ^ reach) for d in range(ways)])  70.5 us
    all_gather x1, waiting for transfers between devices, on_device(): lax.all_gather(w_down, 'dp', axis=1, tiled=True)  41.5 us
    unnamed x51, local copies, waits for them, and re-layouts  30 us
  transfers between devices with their start and end apart: 12, of which 11 were waited for; matrix products, arithmetic and copies ran while one was open for 16% of the time, Pallas kernels for 0%

profile of v1, /device:TPU:0, one launch (start us, length us, event | category | flops | bytes accessed | tf_op | source)
XLA Modules:
  0.0 655.0 jit_solution(10105229117529455161)
XLA Ops:
  17.0 4.2 all-to-all-start.2
  39.2 35.6 %collective-permute-done.1 = bf16[2,1024,256]{2,1,0:T(8,128)(2,1)} collective-permute-done((bf16[2,1024,256]{2,1,0:T(8,128)(2,1)}, bf16[2,1024,256]{2,1,0:T(8,128)(2,1)}, u32[]{:S(2)}, u32[]{:S(2)}) %collective-permute-start.1) | collective-permute-done | bytes 1048608 | tf_op jit(solution)/shard_map/ppermute | solution.py:14
  74.8 4.2 maximum_select_fusion.1
  89.0 4.2 all-to-all-start
  95.5 9.4 %all-to-all-done = bf16[4,2,48,1024]{3,2,1,0:T(8,128)(2,1)} async-done(((bf16[4,2,48,1024]{3,2,1,0:T(8,128)(2,1)}), bf16[4,2,48,1024]{3,2,1,0:T(8,128)(2,1)}, u32[]{:S(2)}, u32[]{:S(2)}) %all-to-all-start) | async-done | bytes 786464 | tf_op jit(solution)/shard_map/all_to_all | solution.py:92
  107.0 41.5 %all-gather.2.cloned.1.call-done = bf16[2,1024,1024]{2,1,0:T(8,128)(2,1)} async-done(((bf16[2,128,1024]{2,1,0:T(8,128)(2,1)}), bf16[2,1024,1024]{2,1,0:T(8,128)(2,1)}) %all-gather.2.cloned.1.call-update) | async-done | bytes 4194320 | tf_op jit(solution)/shard_map/all_gather | solution.py:96
  148.5 4.0 fusion.68
  152.6 33.6 %collective-permute-done.2 = bf16[2,1024,512]{2,1,0:T(8,128)(2,1)} collective-permute-done((bf16[2,1024,512]{2,1,0:T(8,128)(2,1)}, bf16[2,1024,512]{2,1,0:T(8,128)(2,1)}, u32[]{:S(2)}, u32[]{:S(2)}) %collective-permute-start.2) | collective-permute-done | bytes 2097184 | tf_op jit(solution)/shard_map/ppermute | solution.py:14
  186.2 6.4 fusion.6
  196.9 11.3 %copy.64 = bf16[2,1024,1024]{1,0,2:T(2,128)(2,1)} copy(bf16[2,1024,1024]{2,1,0:T(8,128)(2,1)} %convolution_convert_fusion.1) | data formatting | bytes 8388608
  208.2 5.7 copy.73
  214.0 5.0 convolution_convert_fusion
  219.0 5.3 fusion.9
  226.0 4.2 all-to-all-start.3
  230.2 3.9 fusion.8
  235.8 6.1 all-to-all-done.3
  241.9 4.2 all-to-all-start.1
  248.6 9.2 %all-to-all-done.1 = bf16[1,2,192,1024]{3,1,0,2:T(2,128)(2,1)} async-done(((bf16[1,2,192,1024]{3,1,0,2:T(2,128)(2,1)}), bf16[1,2,192,1024]{3,1,0,2:T(2,128)(2,1)}, u32[]{:S(2)}, u32[]{:S(2)}) %all-to-all-start.1) | async-done | bytes 786464 | tf_op jit(solution)/shard_map/all_to_all | solution.py:102
  263.6 3.6 gather_fusion
  285.9 3.7 fusion.32
  293.3 6.9 %reduce-scatter.13.cloned.1.call-done = bf16[128,2048]{1,0:T(8,128)(2,1)} async-done(((bf16[1024,2048]{1,0:T(8,128)(2,1)}), bf16[128,2048]{1,0:T(8,128)(2,1)}) %reduce-scatter.13.cloned.1.call-update) | async-done | bytes 524304
  306.5 85.4 %reduce-scatter.11.cloned.1.call-done = bf16[2,128,1024]{2,1,0:T(8,128)(2,1)} async-done(((bf16[2,1024,1024]{2,1,0:T(8,128)(2,1)}), bf16[2,128,1024]{2,1,0:T(8,128)(2,1)}) %reduce-scatter.11.cloned.1.call-update) | async-done | bytes 524304 | tf_op jit(solution)/shard_map/reduce_scatter | solution.py:119
  394.1 137.2 %reduce-scatter.9.cloned.1.call-done = f32[32,512]{1,0:T(8,128)} async-done(((f32[1024,512]{1,0:T(8,128)}), f32[32,512]{1,0:T(8,128)}) %reduce-scatter.9.cloned.1.call-update) | async-done | bytes 65552 | tf_op jit(solution)/shard_map/reduce_scatter | solution.py:130
  531.2 117.3 %reduce-scatter.7.cloned.1.call-done = f32[32,1536]{1,0:T(8,128)} async-done(((f32[1024,1536]{1,0:T(8,128)}), f32[32,1536]{1,0:T(8,128)}) %reduce-scatter.7.cloned.1.call-update) | async-done | bytes 196624 | tf_op jit(solution)/shard_map/reduce_scatter | solution.py:129
  (116 shorter events, 88.8 us)
Async XLA Ops:
  7.2 20.9 %copy-start = (bf16[1024,1536]{1,0:T(8,128)(2,1)S(1)}, bf16[1024,1536]{1,0:T(8,128)(2,1)}, u32[]{:S(2)}) copy-start(bf16[1024,1536]{1,0:T(8,128)(2,1)} %param.11) | copy-start | bytes 9437188
  7.2 141.4 %all-gather.2.cloned.1.call-start = ((), (), s32[]{:S(2)}) async-start(), calls=%async_computation.8 | async-start | bytes 4718592 | tf_op jit(solution)/shard_map/all_gather | solution.py:96
  7.9 15.9 %collective-permute-start = (bf16[2,1024,128]{2,1,0:T(8,128)(2,1)}, bf16[2,1024,128]{2,1,0:T(8,128)(2,1)}, u32[]{:S(2)}, u32[]{:S(2)}) collective-permute-start(bf16[2,1024,128]{2,1,0:T(8,128)(2,1)} %param.13), channel_id=1, source_target_pairs={{0,4},{4,0},{8,12},{12,8},{16,20},{20,16},{24,28},{28,24},{1,5},{5... | collective-permute-start | bytes 1572872 | tf_op jit(solution)/shard_map/ppermute | solution.py:14
  17.0 72.0 %all-to-all-start.2 = ((bf16[4,2,48,1024]{3,2,1,0:T(8,128)(2,1)}), bf16[4,2,48,1024]{3,2,1,0:T(8,128)(2,1)}, u32[]{:S(2)}, u32[]{:S(2)}) async-start(bf16[4,2,48,1024]{3,2,1,0:T(8,128)(2,1)} %bitcast.119), calls=%async_computation.2 | async-start | bytes 1572864 | tf_op jit(solution)/shard_map/all_to_all | solution.py:105
  21.2 6.8 %copy-start.3 = (bf16[256,1024]{1,0:T(8,128)(2,1)S(1)}, bf16[256,1024]{1,0:T(8,128)(2,1)}, u32[]{:S(2)}) copy-start(bf16[256,1024]{1,0:T(8,128)(2,1)} %param.8) | copy-start | bytes 1572868
  26.8 48.0 %collective-permute-start.1 = (bf16[2,1024,256]{2,1,0:T(8,128)(2,1)}, bf16[2,1024,256]{2,1,0:T(8,128)(2,1)}, u32[]{:S(2)}, u32[]{:S(2)}) collective-permute-start(bf16[2,1024,256]{2,1,0:T(8,128)(2,1)} %maximum_select_fusion.2), channel_id=1, source_target_pairs={{0,8},{4,12},{8,0},{12,4},{16,24},{20,28},{24,16},{28,20},{1,9},{5... | collective-permute-start | bytes 3145736 | tf_op jit(solution)/shard_map/ppermute | solution.py:14
  33.1 6.0 copy-start.21
  37.0 42.0 %copy-start.17 = (bf16[2,128,1,8,64]{1,4,3,0,2:T(8,128)(2,1)}, bf16[2,128,1,8,64]{1,4,3,0,2:T(8,128)(2,1)S(1)}, u32[]{:S(2)}) copy-start(bf16[2,128,1,8,64]{1,4,3,0,2:T(8,128)(2,1)S(1)} %copy.70) | copy-start | bytes 786436
  39.2 39.7 %copy-start.19 = (bf16[2,128,1,8,64]{1,4,3,0,2:T(8,128)(2,1)S(1)}, bf16[2,128,1,8,64]{1,4,3,0,2:T(8,128)(2,1)}, u32[]{:S(2)}) copy-start(bf16[2,128,1,8,64]{1,4,3,0,2:T(8,128)(2,1)} %copy.69) | copy-start | bytes 786436
  78.9 107.3 %collective-permute-start.2 = (bf16[2,1024,512]{2,1,0:T(8,128)(2,1)}, bf16[2,1024,512]{2,1,0:T(8,128)(2,1)}, u32[]{:S(2)}, u32[]{:S(2)}) collective-permute-start(bf16[2,1024,512]{2,1,0:T(8,128)(2,1)} %maximum_select_fusion.1), channel_id=1, source_target_pairs={{0,16},{4,20},{8,24},{12,28},{16,0},{20,4},{24,8},{28,12},{1,17},{... | collective-permute-start | bytes 6291464 | tf_op jit(solution)/shard_map/ppermute | solution.py:14
  81.7 2.9 copy-start.4
  81.7 2.9 copy-start.13
  89.0 15.9 %all-to-all-start = ((bf16[4,2,48,1024]{3,2,1,0:T(8,128)(2,1)}), bf16[4,2,48,1024]{3,2,1,0:T(8,128)(2,1)}, u32[]{:S(2)}, u32[]{:S(2)}) async-start(bf16[4,2,48,1024]{3,2,1,0:T(8,128)(2,1)} %bitcast.120), calls=%async_computation | async-start | bytes 1572864 | tf_op jit(solution)/shard_map/all_to_all | solution.py:92
  93.2 207.0 %reduce-scatter.13.cloned.1.call-start = ((), (), s32[]{:S(2)}) async-start(), calls=%async_computation.12 | async-start | bytes 4718592
  148.5 37.7 %copy-start.10 = (bf16[1,2,4,48,1024]{4,3,2,1,0:T(8,128)(2,1)S(1)}, bf16[1,2,4,48,1024]{4,3,2,1,0:T(8,128)(2,1)}, u32[]{:S(2)}) copy-start(bf16[1,2,4,48,1024]{4,3,2,1,0:T(8,128)(2,1)} %copy.47) | copy-start | bytes 2359300
  213.9 178.0 %reduce-scatter.11.cloned.1.call-start = ((), (), s32[]{:S(2)}) async-start(), calls=%async_computation.11 | async-start | bytes 4718592 | tf_op jit(solution)/shard_map/reduce_scatter | solution.py:119
  226.0 15.9 %all-to-all-start.3 = ((bf16[1,2,192,1024]{3,1,0,2:T(2,128)(2,1)}), bf16[1,2,192,1024]{3,1,0,2:T(2,128)(2,1)}, u32[]{:S(2)}, u32[]{:S(2)}) async-start(bf16[1,2,192,1024]{3,1,0,2:T(2,128)(2,1)} %copy.51), calls=%async_computation.3 | async-start | bytes 1572864 | tf_op jit(solution)/shard_map/all_to_all | solution.py:113
  241.9 15.9 %all-to-all-start.1 = ((bf16[1,2,192,1024]{3,1,0,2:T(2,128)(2,1)}), bf16[1,2,192,1024]{3,1,0,2:T(2,128)(2,1)}, u32[]{:S(2)}, u32[]{:S(2)}) async-start(bf16[1,2,192,1024]{3,1,0,2:T(2,128)(2,1)} %copy.48), calls=%async_computation.1 | async-start | bytes 1572864 | tf_op jit(solution)/shard_map/all_to_all | solution.py:102
  246.1 285.1 %reduce-scatter.9.cloned.1.call-start = ((), (), s32[]{:S(2)}) async-start(), calls=%async_computation.10 | async-start | bytes 2162688 | tf_op jit(solution)/shard_map/reduce_scatter | solution.py:130
  267.3 5.0 copy-start.15
  274.1 374.4 %reduce-scatter.7.cloned.1.call-start = ((), (), s32[]{:S(2)}) async-start(), calls=%async_computation.9 | async-start | bytes 6488064 | tf_op jit(solution)/shard_map/reduce_scatter | solution.py:129
  280.2 2.4 copy-start.18
  289.6 2.5 copy-start.2
  289.6 2.5 copy-start.6
  (10 other events, 13.6 us)
Sparse Core Ops, SparseCore 0:
  10.2 138.2 all-gather.1
  214.1 86.0 reduce-scatter.12
  304.3 87.6 reduce-scatter.10
  394.6 136.5 reduce-scatter.8
  538.2 110.2 reduce-scatter.6
